TPU v7x, 512 devices: a whole 4x4x16 slice. The times are simulated.
512 devices in a mesh: pipe: 2 (over z_hi), ctx: 64 (over y, z_lo, core), tp: 4 (over x).
Axes of the slice: x: 4, y: 4, z: 16 (z_hi: 2, z_lo: 8; z = z_hi * 8 + z_lo), core: 2. Of those that a mesh axis runs over, the one named last changes fastest.
Arguments:
- section_output: bfloat16 [2, 8192, 8192], P('pipe', 'ctx', 'tp'), may hold values from -26 to 26
- norm_gain: float32 [2, 8192], P('pipe'), may hold values from 0.1 to 1.9
- kv_weight: bfloat16 [2, 8192, 1024], P('pipe', 'ctx', 'tp'), may hold values from -0.0625 to 0.0625
- queries: bfloat16 [2, 8192, 4096], P('pipe', 'ctx', 'tp'), may hold values from -171 to 171
- rank_block: int32 [128], replicated, may hold values from 0 to 127, each once
Outputs:
- attention: bfloat16 [2, 8192, 4096], P('pipe', 'ctx', 'tp')
- log_total: float32 [2, 8192, 32], P('pipe', 'ctx', 'tp')
Inputs may be any that keep to these rules, and one draw needn't show every extreme that they name: `rank_block`: each of 0 to 127 once.
All inputs are finite; a program needn't handle non-finite values.
Results may differ from a plain program's by a relative error of at most 0.017.
The roundings to bfloat16 on the way count: a program that leaves them out, or rounds other values in their place, can miss the bound.
Values may be sent and summed in bfloat16 or wider, within the bound.
No kernel may reach another device: no remote copies, remote signals or barrier semaphores. Data moves between devices by JAX's collectives and lax.ppermute only.
A program may use at most 128 MiB of HBM per device.

v0:
```python
import math
import jax
import jax.numpy as jnp
from jax import lax
from jax.sharding import PartitionSpec as P

HD = 128
norm_eps = 1e-05
rope_base = 500000.0
mask_fill = -1e30


def passed_along(shard, axis, by):
    peers = lax.axis_size(axis)
    return lax.ppermute(shard, axis, [(i, (i + by) % peers) for i in range(peers)])


def block_positions(rank_block, ctx_count, half_rows):
    block_ids = rank_block.reshape(ctx_count, 2)
    within = jnp.arange(half_rows, dtype=jnp.int32)
    return (block_ids[:, :, None] * half_rows + within[None, None, :]).reshape(-1)


def rotate_keys(raw_keys, positions):
    width = raw_keys.shape[-1]
    half_width = width // 2
    steps_f = jnp.arange(half_width, dtype=jnp.float32)
    inv_freq = jnp.exp(steps_f * (-2.0 / width) * math.log(rope_base))
    angles = positions.astype(jnp.float32)[:, None] * inv_freq[None, :]
    cosine = jnp.cos(angles)
    sine_part = jnp.sin(angles)
    first_half = raw_keys[:, :half_width]
    second_half = raw_keys[:, half_width:]
    return jnp.concatenate(
        [
            first_half * cosine - second_half * sine_part,
            second_half * cosine + first_half * sine_part,
        ],
        axis=1,
    )


def body(section_output, norm_gain, kv_weight, queries, rank_block):
    ctx_count = lax.axis_size("ctx")
    tok_rows = section_output.shape[1]
    half_rows = tok_rows // 2
    head_dim = HD
    head_count = queries.shape[2] // head_dim
    score_scale = 1.0 / math.sqrt(head_dim)
    received = passed_along(section_output, "pipe", 1)
    gathered = lax.all_gather(received, "tp", axis=2, tiled=True)[0].astype(jnp.float32)
    mean_sq = jnp.mean(gathered * gathered, axis=-1, keepdims=True)
    normed = (gathered * lax.rsqrt(mean_sq + norm_eps) * norm_gain[0]).astype(jnp.bfloat16)
    projected = jnp.dot(
        normed,
        lax.all_gather(kv_weight, "ctx", axis=1, tiled=True)[0],
        preferred_element_type=jnp.float32,
    )
    all_pos = block_positions(rank_block, ctx_count, half_rows)
    own_pos = lax.dynamic_slice_in_dim(all_pos, lax.axis_index("ctx") * tok_rows, tok_rows)
    keys = rotate_keys(projected[:, :head_dim], own_pos).astype(jnp.bfloat16)
    values = projected[:, head_dim:].astype(jnp.bfloat16)
    key_values = jnp.concatenate([keys, values], axis=1)
    query_rows = queries[0].reshape(tok_rows, head_count, head_dim)
    halves = (
        (query_rows[:half_rows], own_pos[:half_rows]),
        (query_rows[half_rows:], own_pos[half_rows:]),
    )

    def tile_logits(query_part, query_pos, segment, key_pos):
        logits = (
            jnp.einsum(
                "qhd,kd->hqk", query_part, segment[:, :head_dim], preferred_element_type=jnp.float32
            )
            * score_scale
        )
        allowed = key_pos[None, None, :] <= query_pos[None, :, None]
        return (logits, allowed)

    def weighted_sum(att_weights, segment):
        return jnp.einsum(
            "hqk,kd->qhd",
            att_weights,
            segment[:, head_dim:].astype(jnp.float32),
            precision=lax.Precision.HIGHEST,
        )

    start_pair = (
        jnp.full((head_count, half_rows), mask_fill, jnp.float32),
        jnp.zeros((head_count, half_rows), jnp.float32),
    )
    init_totals = (start_pair, start_pair)
    start_accum = jnp.zeros((half_rows, head_count, head_dim), jnp.float32)
    init_outputs = (start_accum, start_accum)
    segment = lax.all_gather(key_values, "ctx", axis=0, tiled=True)
    key_pos = all_pos
    results = []
    for half_idx in range(2):
        query_part, query_pos = halves[half_idx]

        def update(state_in, query_part=query_part, query_pos=query_pos):
            logits, allowed = tile_logits(query_part, query_pos, segment, key_pos)
            logits = jnp.where(allowed, logits, mask_fill)
            row_max = jnp.maximum(state_in[0], jnp.max(logits, axis=-1))
            row_sum = jnp.sum(jnp.exp(logits - row_max[..., None]), axis=-1)
            return (row_max, row_sum)

        results.append(update(init_totals[half_idx]))
    totals = tuple(results)
    log_halves = tuple((running_pair[0] + jnp.log(running_pair[1]) for running_pair in totals))
    output_segment = lax.all_gather(key_values, "ctx", axis=0, tiled=True)
    results = []
    for half_idx in range(2):
        query_part, query_pos = halves[half_idx]
        log_half = log_halves[half_idx]

        def update(accum, query_part=query_part, query_pos=query_pos, log_half=log_half):
            logits, allowed = tile_logits(query_part, query_pos, output_segment, all_pos)
            att_weights = jnp.where(allowed, jnp.exp(logits - log_half[..., None]), 0.0)
            return weighted_sum(att_weights, output_segment)

        results.append(update(init_outputs[half_idx]))
    outputs = tuple(results)
    attention = (
        jnp.concatenate(outputs, axis=0)
        .astype(jnp.bfloat16)
        .reshape(tok_rows, head_count * head_dim)
    )
    log_total = jnp.concatenate(
        [jnp.transpose(log_halves[0]), jnp.transpose(log_halves[1])], axis=0
    )
    return (attention[None], log_total[None])


def solution(mesh):
    return jax.shard_map(
        body,
        mesh=mesh,
        in_specs=(
            P("pipe", "ctx", "tp"),
            P("pipe", None),
            P("pipe", "ctx", "tp"),
            P("pipe", "ctx", "tp"),
            P(),
        ),
        out_specs=(P("pipe", "ctx", "tp"), P("pipe", "ctx", "tp")),
        check_vma=False,
    )
```

profile of v0, /device:TPU:1, one launch (start us, length us, event | category | flops | bytes accessed | tf_op | source)
XLA Modules:
  0.0 424.6 jit_solution(8950425790996297745)
XLA Ops:
  7.2 16.3 %collective-permute-start = (bf16[1,128,2048]{2,1,0:T(8,128)(2,1)}, bf16[1,128,2048]{2,1,0:T(8,128)(2,1)S(1)}, u32[]{:S(2)}, u32[]{:S(2)}) collective-permute-start(bf16[1,128,2048]{2,1,0:T(8,128)(2,1)} %param.5), channel_id=1, source_target_pairs={{0,256},{256,0},{1,257},{257,1},{2,258},{258,2},{3,259},{259,3},{4... | collective-permute-start | bytes 1572872 | tf_op jit(solution)/shard_map/ppermute | solution.py:15
  23.5 15.2 %collective-permute-done = bf16[1,128,2048]{2,1,0:T(8,128)(2,1)S(1)} collective-permute-done((bf16[1,128,2048]{2,1,0:T(8,128)(2,1)}, bf16[1,128,2048]{2,1,0:T(8,128)(2,1)S(1)}, u32[]{:S(2)}, u32[]{:S(2)}) %collective-permute-start) | collective-permute-done | bytes 524320 | tf_op jit(solution)/shard_map/ppermute | solution.py:15
  38.7 0.8 copy-done.1
  39.6 0.7 all-gather.6.cloned.1.call-update
  40.3 0.7 broadcast_multiply_fusion
  41.0 0.1 mul.100
  41.1 0.1 iota_add_fusion
  41.5 68.4 %all-gather.4.cloned.1.call-done = bf16[1,128,8192]{2,1,0:T(8,128)(2,1)} async-done(((bf16[1,128,2048]{2,1,0:T(8,128)(2,1)}), bf16[1,128,8192]{2,1,0:T(8,128)(2,1)}) %all-gather.4.cloned.1.call-update) | async-done | bytes 2097168 | tf_op jit(solution)/shard_map/all_gather | solution.py:51
  109.8 2.1 fusion.20
  111.9 123.5 %all-gather.6.cloned.1.call-done = bf16[1,8192,256]{2,1,0:T(8,128)(2,1)} async-done(((bf16[1,128,256]{2,1,0:T(8,128)(2,1)}), bf16[1,8192,256]{2,1,0:T(8,128)(2,1)}) %all-gather.6.cloned.1.call-update) | async-done | bytes 4194320 | tf_op jit(solution)/shard_map/all_gather | solution.py:56
  235.4 3.6 fusion.23
  239.3 0.2 fusion.50
  239.6 0.1 copy.14
  239.7 0.7 pad_maximum_fusion.1
  240.5 1.0 slice_bitcast_fusion.15
  241.6 0.6 broadcast_compare_fusion.1
  242.3 116.9 %all-gather.8.cloned.1.call-done = bf16[8192,256]{1,0:T(8,128)(2,1)} async-done(((bf16[128,256]{1,0:T(8,128)(2,1)}), bf16[8192,256]{1,0:T(8,128)(2,1)}) %all-gather.8.cloned.1.call-update) | async-done | bytes 4194320 | tf_op jit(solution)/shard_map/all_gather | solution.py:111
  359.2 9.1 %fusion.8 = (f32[8,64]{1,0:T(8,128)S(1)}, f32[8192,64,8]{0,1,2:T(8,128)}) fusion(pred[64,8192]{1,0:T(8,128)(4,1)S(1)} %get-tuple-element.10, bf16[64,8,128]{2,1,0:T(8,128)(2,1)S(1)} %bitcast.76, bf16[8192,256]{1,0:T(8,128)(2,1)} %all-gather.8.cloned.1.call-done), kind=kOutput, calls=%fused_computation.12 | convolution fusion | flops 1086324224 | bytes 19531776 | tf_op jit(solution)/shard_map/qhd,kd->hqk/dot_general | solution.py:72
  368.3 3.1 fusion.9
  371.4 16.4 %exponential_reduce_fusion = (f32[8,64]{1,0:T(8,128)S(1)}, f32[8,64]{1,0:T(8,128)S(1)}) fusion(f32[8192,64,8]{0,1,2:T(8,128)S(1)} %get-tuple-element.15, f32[8,64]{1,0:T(8,128)S(1)} %broadcast_maximum_fusion, pred[64,8192]{1,0:T(8,128)(4,1)S(1)} %get-tuple-element.11, f32[8,64]{1,0:T(8,128)S(1)} %broadcast_maximum_fusion.1, ...), kind=kLoop, calls=%fused_computation.10 | loop fusion | flops 33553408 | bytes 34611200 | tf_op jit(solution)/shard_map/reduce_sum | solution.py:105
  387.8 14.0 %fusion.40 = bf16[64,8,128]{2,0,1:T(8,128)(2,1)S(1)} fusion(f32[8192,64,8]{0,1,2:T(8,128)} %get-tuple-element.17, f32[8,64]{1,0:T(8,128)S(1)} %log_add_fusion.1, pred[64,8192]{1,0:T(8,128)(4,1)S(1)} %get-tuple-element.10, bf16[8192,256]{1,0:T(8,128)(2,1)S(1)} %copy-done.2), kind=kOutput, calls=%fused_computation.41 | convolution fusion | flops 6455099392 | bytes 19533824 | tf_op jit(solution)/shard_map/hqk,kd->qhd/dot_general | solution.py:81
  402.1 14.4 %fusion.37 = bf16[64,8,128]{2,0,1:T(8,128)(2,1)S(1)} fusion(f32[8192,64,8]{0,1,2:T(8,128)} %copy-done, f32[8,64]{1,0:T(8,128)S(1)} %log_add_fusion, pred[64,8192]{1,0:T(8,128)(4,1)S(1)} %get-tuple-element.11, bf16[8192,256]{1,0:T(8,128)(2,1)} %all-gather.8.cloned.1.call-done), kind=kOutput, calls=%fused_computation.40 | convolution fusion | flops 6455099392 | bytes 19531776 | tf_op jit(solution)/shard_map/hqk,kd->qhd/dot_general | solution.py:81
  416.7 0.7 pad_maximum_fusion
  417.4 0.7 maximum_bitcast_fusion
  (30 shorter events, 1.1 us)
Async XLA Ops:
  7.2 102.7 %all-gather.4.cloned.1.call-start = ((), (), s32[]{:S(2)}) async-start(), calls=%async_computation | async-start | bytes 2621440 | tf_op jit(solution)/shard_map/all_gather | solution.py:51
  7.2 31.5 %collective-permute-start = (bf16[1,128,2048]{2,1,0:T(8,128)(2,1)}, bf16[1,128,2048]{2,1,0:T(8,128)(2,1)S(1)}, u32[]{:S(2)}, u32[]{:S(2)}) collective-permute-start(bf16[1,128,2048]{2,1,0:T(8,128)(2,1)} %param.5), channel_id=1, source_target_pairs={{0,256},{256,0},{1,257},{257,1},{2,258},{258,2},{3,259},{259,3},{4... | collective-permute-start | bytes 1572872 | tf_op jit(solution)/shard_map/ppermute | solution.py:15
  38.7 0.8 copy-start.1
  39.5 195.9 %all-gather.6.cloned.1.call-start = ((), (), s32[]{:S(2)}) async-start(), calls=%async_computation.1 | async-start | bytes 4259840 | tf_op jit(solution)/shard_map/all_gather | solution.py:56
  40.3 318.9 %all-gather.8.cloned.1.call-start = ((), (), s32[]{:S(2)}) async-start(), calls=%async_computation.2 | async-start | bytes 4259840 | tf_op jit(solution)/shard_map/all_gather | solution.py:111
  359.2 9.1 %copy-start.2 = (bf16[8192,256]{1,0:T(8,128)(2,1)S(1)}, bf16[8192,256]{1,0:T(8,128)(2,1)}, u32[]{:S(2)}) copy-start(bf16[8192,256]{1,0:T(8,128)(2,1)} %all-gather.8.cloned.1.call-done) | copy-start | bytes 12582916
  371.4 16.4 %copy-start = (f32[8192,64,8]{0,1,2:T(8,128)}, f32[8192,64,8]{0,1,2:T(8,128)S(1)}, u32[]{:S(2)}) copy-start(f32[8192,64,8]{0,1,2:T(8,128)S(1)} %get-tuple-element.15) | copy-start | bytes 50331652
Sparse Core Ops, SparseCore 0:
  39.7 70.1 all-gather.3
  112.0 123.3 all-gather.5
  240.6 118.5 all-gather.7
where the time goes:
time: 425 us
  waiting for transfers between devices  325 us (76%)
  matrix products  44.3 us (10%)
  other arithmetic  22.4 us (5%)
  starting transfers between devices  16.4 us (4%)
  between operations  13.9 us (3%)
    all_gather x1, waiting for transfers between devices, body(): lax.all_gather(kv_weight, 'ctx', axis=1, tiled=True)[0]  123 us
    all_gather x1, waiting for transfers between devices, body(): output_segment = lax.all_gather(key_values, 'ctx', axis=0, tiled=True)  117 us
    all_gather x1, waiting for transfers between devices, body(): lax.all_gather(received, 'tp', axis=2, tiled=True)[0].astype(jnp.float32)  68.4 us
    dot_general x2, matrix products, weighted_sum(): jnp.einsum('hqk,kd->qhd', att_weights, segment[:, head_dim:].astype(jnp.f...  28.5 us
    reduce_sum x1, other arithmetic, update(): row_sum = jnp.sum(jnp.exp(logits - row_max[..., None]), axis=-1)  16.4 us
    ppermute x1, starting transfers between devices, passed_along(): lax.ppermute(shard, axis, [(i, (i + by) % peers) for i in range(peers)])  16.3 us
    ppermute x1, waiting for transfers between devices, passed_along(): lax.ppermute(shard, axis, [(i, (i + by) % peers) for i in range(peers)])  15.2 us
    dot_general x2, matrix products, tile_logits(): jnp.einsum('qhd,kd->hqk', query_part, segment[:, :head_dim], preferred_el...  12.2 us
  transfers between devices with their start and end apart: 4, of which 4 were waited for; matrix products, arithmetic and copies ran while one was open for 1% of the time, Pallas kernels for 0%

commit v1 on v0

--- a/solution.py
+++ b/solution.py
@@ -1,3 +1,4 @@
+import functools
 import math
 import jax
 import jax.numpy as jnp
@@ -8,6 +9,37 @@
 norm_eps = 1e-05
 rope_base = 500000.0
 mask_fill = -1e30
+
+
+def weights_test(array_in, array_axis):
+    then, before, left_arr = (lax.axis_size("tp"), lax.axis_index("tp"), array_in.shape[array_axis])
+    all_blocks = []
+    for t, j in enumerate(array_in.shape):
+        all_blocks.append(j * then if t == array_axis else j)
+    passed = arr_now = array_in
+    placed = lax.dynamic_update_slice_in_dim(
+        jnp.zeros(all_blocks, array_in.dtype), array_in, before * left_arr, axis=array_axis
+    )
+    for no in [*range(1, then // 2 + 1)]:
+        made = []
+        for t in tuple(range(then)):
+            made.append((t, (t + 1) % then))
+        passed = lax.ppermute(passed, axis_name="tp", perm=made)
+        placed = lax.dynamic_update_slice_in_dim(
+            placed, passed, (before - no) % then * left_arr, axis=array_axis
+        )
+        if 2 * no < then:
+            column = []
+            for t in [*range(then)]:
+                column.append((t, (t - 1) % then))
+            arr_now = lax.ppermute(arr_now, axis_name="tp", perm=column)
+            placed = lax.dynamic_update_slice_in_dim(
+                placed, arr_now, (before + no) % then * left_arr, axis=array_axis
+            )
+    return placed
+
+
+seats_all_resolve = functools.partial(weights_test, array_axis=2)
 
 
 def passed_along(shard, axis, by):
@@ -48,7 +80,7 @@
     head_count = queries.shape[2] // head_dim
     score_scale = 1.0 / math.sqrt(head_dim)
     received = passed_along(section_output, "pipe", 1)
-    gathered = lax.all_gather(received, "tp", axis=2, tiled=True)[0].astype(jnp.float32)
+    gathered = seats_all_resolve(received)[0].astype(jnp.float32)
     mean_sq = jnp.mean(gathered * gathered, axis=-1, keepdims=True)
     normed = (gathered * lax.rsqrt(mean_sq + norm_eps) * norm_gain[0]).astype(jnp.bfloat16)
     projected = jnp.dot(

time: 425 us -> 357 us (0.84)
  waiting for transfers between devices: 325 us -> 253 us
  starting transfers between devices: 16.4 us -> 24.7 us
  other arithmetic: 22.4 us -> 16 us
    all_gather x1 -> x0, waiting for transfers between devices: 68.4 us -> none  [body(): lax.all_gather(received, 'tp', axis=2, tiled=True)[0].astype(jnp.float32)]
    all_gather x1, waiting for transfers between devices: 123 us -> 106 us  [body(): lax.all_gather(kv_weight, 'ctx', axis=1, tiled=True)[0]]
    ppermute x0 -> x3, waiting for transfers between devices: none -> 13.4 us  [the longest x2 12.9 us: weights_test(): passed = lax.ppermute(passed, axis_name='tp', perm=made)]
    ppermute x0 -> x3, starting transfers between devices: none -> 8.39 us  [the longest x2 5.02 us: weights_test(): passed = lax.ppermute(passed, axis_name='tp', perm=made)]
    reduce_sum x1, other arithmetic: 16.4 us -> 11.6 us  [update(): row_sum = jnp.sum(jnp.exp(logits - row_max[..., None]), axis=-1)]
  transfers between devices with their start and end apart: 4 -> 6, of which waited for: 4 -> 6; matrix products, arithmetic and copies ran while one was open for 1% -> 1% of each run, Pallas kernels for 0% -> 0%
where the time goes in v1:
time: 357 us
  waiting for transfers between devices  253 us (71%)
  matrix products  44.3 us (12%)
  starting transfers between devices  24.7 us (7%)
  other arithmetic  16 us (4%)
  between operations  14.4 us (4%)
  local copies, waits for them, and re-layouts  4.47 us (1%)
    all_gather x1, waiting for transfers between devices, body(): output_segment = lax.all_gather(key_values, 'ctx', axis=0, tiled=True)  117 us
    all_gather x1, waiting for transfers between devices, body(): lax.all_gather(kv_weight, 'ctx', axis=1, tiled=True)[0]  106 us
    dot_general x2, matrix products, weighted_sum(): jnp.einsum('hqk,kd->qhd', att_weights, segment[:, head_dim:].astype(jnp.f...  28.7 us
    ppermute x1, starting transfers between devices, passed_along(): lax.ppermute(shard, axis, [(i, (i + by) % peers) for i in range(peers)])  16.3 us
    ppermute x1, waiting for transfers between devices, passed_along(): lax.ppermute(shard, axis, [(i, (i + by) % peers) for i in range(peers)])  15.5 us
    ppermute x2, waiting for transfers between devices, weights_test(): passed = lax.ppermute(passed, axis_name='tp', perm=made)  12.9 us
    dot_general x2, matrix products, tile_logits(): jnp.einsum('qhd,kd->hqk', query_part, segment[:, :head_dim], preferred_el...  12.6 us
    reduce_sum x1, other arithmetic, update(): row_sum = jnp.sum(jnp.exp(logits - row_max[..., None]), axis=-1)  11.6 us
  transfers between devices with their start and end apart: 6, of which 6 were waited for; matrix products, arithmetic and copies ran while one was open for 1% of the time, Pallas kernels for 0%

profile of v1, /device:TPU:1, one launch (start us, length us, event | category | flops | bytes accessed | tf_op | source)
XLA Modules:
  0.0 356.8 jit_solution(10648757309520072343)
XLA Ops:
  7.2 0.7 all-gather.3.cloned.1.call-update
  7.9 16.3 %collective-permute-start = (bf16[1,128,2048]{2,1,0:T(8,128)(2,1)}, bf16[1,128,2048]{2,1,0:T(8,128)(2,1)S(1)}, u32[]{:S(2)}, u32[]{:S(2)}) collective-permute-start(bf16[1,128,2048]{2,1,0:T(8,128)(2,1)} %param.5), channel_id=1, source_target_pairs={{0,256},{256,0},{1,257},{257,1},{2,258},{258,2},{3,259},{259,3},{4... | collective-permute-start | bytes 1572872 | tf_op jit(solution)/shard_map/ppermute | solution.py:47
  24.2 0.7 broadcast_multiply_fusion
  25.3 15.5 %collective-permute-done = bf16[1,128,2048]{2,1,0:T(8,128)(2,1)S(1)} collective-permute-done((bf16[1,128,2048]{2,1,0:T(8,128)(2,1)}, bf16[1,128,2048]{2,1,0:T(8,128)(2,1)S(1)}, u32[]{:S(2)}, u32[]{:S(2)}) %collective-permute-start) | collective-permute-done | bytes 524320 | tf_op jit(solution)/shard_map/ppermute | solution.py:47
  40.8 3.1 collective-permute-start.1
  44.0 3.4 collective-permute-start.2
  47.7 4.3 %collective-permute-done.1 = bf16[1,128,2048]{2,1,0:T(8,128)(2,1)S(1)} collective-permute-done((bf16[1,128,2048]{2,1,0:T(8,128)(2,1)S(1)}, bf16[1,128,2048]{2,1,0:T(8,128)(2,1)S(1)}, u32[]{:S(2)}, u32[]{:S(2)}) %collective-permute-start.1) | collective-permute-done | bytes 524320 | tf_op jit(solution)/shard_map/ppermute | solution.py:27
  52.0 1.9 collective-permute-start.3
  53.9 0.4 collective-permute-done.2
  54.4 8.7 %collective-permute-done.3 = bf16[1,128,2048]{2,1,0:T(8,128)(2,1)S(1)} collective-permute-done((bf16[1,128,2048]{2,1,0:T(8,128)(2,1)S(1)}, bf16[1,128,2048]{2,1,0:T(8,128)(2,1)S(1)}, u32[]{:S(2)}, u32[]{:S(2)}) %collective-permute-start.3) | collective-permute-done | bytes 524320 | tf_op jit(solution)/shard_map/ppermute | solution.py:27
  63.1 0.5 fusion.20
  63.7 106.5 %all-gather.3.cloned.1.call-done = bf16[1,8192,256]{2,1,0:T(8,128)(2,1)} async-done(((bf16[1,128,256]{2,1,0:T(8,128)(2,1)}), bf16[1,8192,256]{2,1,0:T(8,128)(2,1)}) %all-gather.3.cloned.1.call-update) | async-done | bytes 4194320 | tf_op jit(solution)/shard_map/all_gather | solution.py:88
  170.1 3.0 fusion.23
  173.9 0.7 pad_maximum_fusion.1
  174.8 0.6 broadcast_compare_fusion.1
  175.5 116.9 %all-gather.5.cloned.1.call-done = bf16[8192,256]{1,0:T(8,128)(2,1)} async-done(((bf16[128,256]{1,0:T(8,128)(2,1)}), bf16[8192,256]{1,0:T(8,128)(2,1)}) %all-gather.5.cloned.1.call-update) | async-done | bytes 4194320 | tf_op jit(solution)/shard_map/all_gather | solution.py:143
  292.4 4.8 %fusion.9 = (f32[8,64]{1,0:T(8,128)S(1)}, f32[8192,64,8]{0,1,2:T(8,128)S(1)}) fusion(pred[64,8192]{1,0:T(8,128)(4,1)S(1)} %get-tuple-element.11, bf16[64,8,128]{2,1,0:T(8,128)(2,1)S(1)} %bitcast.81, bf16[8192,256]{1,0:T(8,128)(2,1)} %all-gather.5.cloned.1.call-done), kind=kOutput, calls=%fused_computation.13 | convolution fusion | flops 1086324224 | bytes 19531776 | tf_op jit(solution)/shard_map/qhd,kd->hqk/dot_general | solution.py:104
  297.2 7.8 %fusion.8 = (f32[8,64]{1,0:T(8,128)S(1)}, f32[8192,64,8]{0,1,2:T(8,128)}) fusion(pred[64,8192]{1,0:T(8,128)(4,1)S(1)} %get-tuple-element.10, bf16[64,8,128]{2,1,0:T(8,128)(2,1)S(1)} %bitcast.80, bf16[8192,256]{1,0:T(8,128)(2,1)S(1)} %copy-done.2), kind=kOutput, calls=%fused_computation.12 | convolution fusion | flops 1086324224 | bytes 19531776 | tf_op jit(solution)/shard_map/qhd,kd->hqk/dot_general | solution.py:104
  305.0 2.9 copy-done
  307.9 11.6 %exponential_reduce_fusion = (f32[8,64]{1,0:T(8,128)S(1)}, f32[8,64]{1,0:T(8,128)S(1)}) fusion(f32[8192,64,8]{0,1,2:T(8,128)S(1)} %get-tuple-element.15, f32[8,64]{1,0:T(8,128)S(1)} %broadcast_maximum_fusion, pred[64,8192]{1,0:T(8,128)(4,1)S(1)} %get-tuple-element.11, f32[8,64]{1,0:T(8,128)S(1)} %broadcast_maximum_fusion.1, ...), kind=kLoop, calls=%fused_computation.10 | loop fusion | flops 33553408 | bytes 34611200 | tf_op jit(solution)/shard_map/reduce_sum | solution.py:137
  319.5 14.0 %fusion.39 = bf16[64,8,128]{2,0,1:T(8,128)(2,1)S(1)} fusion(f32[8192,64,8]{0,1,2:T(8,128)} %get-tuple-element.17, f32[8,64]{1,0:T(8,128)S(1)} %log_add_fusion.1, pred[64,8192]{1,0:T(8,128)(4,1)S(1)} %get-tuple-element.10, bf16[8192,256]{1,0:T(8,128)(2,1)S(1)} %copy-done.2), kind=kOutput, calls=%fused_computation.40 | convolution fusion | flops 6455099392 | bytes 19533824 | tf_op jit(solution)/shard_map/hqk,kd->qhd/dot_general | solution.py:113
  333.7 14.7 %fusion.36 = bf16[64,8,128]{2,0,1:T(8,128)(2,1)S(1)} fusion(f32[8192,64,8]{0,1,2:T(8,128)} %copy-done, f32[8,64]{1,0:T(8,128)S(1)} %log_add_fusion, pred[64,8192]{1,0:T(8,128)(4,1)S(1)} %get-tuple-element.11, bf16[8192,256]{1,0:T(8,128)(2,1)} %all-gather.5.cloned.1.call-done), kind=kOutput, calls=%fused_computation.39 | convolution fusion | flops 6455099392 | bytes 19531776 | tf_op jit(solution)/shard_map/hqk,kd->qhd/dot_general | solution.py:113
  348.6 0.7 pad_maximum_fusion
  349.3 0.7 maximum_bitcast_fusion
  (40 shorter events, 2.1 us)
Async XLA Ops:
  7.2 163.0 %all-gather.3.cloned.1.call-start = ((), (), s32[]{:S(2)}) async-start(), calls=%async_computation | async-start | bytes 4259840 | tf_op jit(solution)/shard_map/all_gather | solution.py:88
  7.9 284.5 %all-gather.5.cloned.1.call-start = ((), (), s32[]{:S(2)}) async-start(), calls=%async_computation.1 | async-start | bytes 4259840 | tf_op jit(solution)/shard_map/all_gather | solution.py:143
  7.9 32.9 %collective-permute-start = (bf16[1,128,2048]{2,1,0:T(8,128)(2,1)}, bf16[1,128,2048]{2,1,0:T(8,128)(2,1)S(1)}, u32[]{:S(2)}, u32[]{:S(2)}) collective-permute-start(bf16[1,128,2048]{2,1,0:T(8,128)(2,1)} %param.5), channel_id=1, source_target_pairs={{0,256},{256,0},{1,257},{257,1},{2,258},{258,2},{3,259},{259,3},{4... | collective-permute-start | bytes 1572872 | tf_op jit(solution)/shard_map/ppermute | solution.py:47
  40.8 11.1 %collective-permute-start.1 = (bf16[1,128,2048]{2,1,0:T(8,128)(2,1)S(1)}, bf16[1,128,2048]{2,1,0:T(8,128)(2,1)S(1)}, u32[]{:S(2)}, u32[]{:S(2)}) collective-permute-start(bf16[1,128,2048]{2,1,0:T(8,128)(2,1)S(1)} %collective-permute-done), channel_id=1, source_target_pairs={{0,1},{1,2},{2,3},{3,0},{4,5},{5,6},{6,7},{7,4},{8,9},{9,10},{10,1... | collective-permute-start | bytes 1572872 | tf_op jit(solution)/shard_map/ppermute | solution.py:27
  44.0 126.1 %copy-start.3 = (f32[1,8192]{1,0:T(1,128)S(1)}, f32[1,8192]{1,0:T(1,128)}, u32[]{:S(2)}) copy-start(f32[1,8192]{1,0:T(1,128)} %param.6) | copy-start | bytes 98308
  44.0 10.3 %collective-permute-start.2 = (bf16[1,128,2048]{2,1,0:T(8,128)(2,1)S(1)}, bf16[1,128,2048]{2,1,0:T(8,128)(2,1)S(1)}, u32[]{:S(2)}, u32[]{:S(2)}) collective-permute-start(bf16[1,128,2048]{2,1,0:T(8,128)(2,1)S(1)} %collective-permute-done), channel_id=1, source_target_pairs={{0,3},{1,0},{2,1},{3,2},{4,7},{5,4},{6,5},{7,6},{8,11},{9,8},{10,9... | collective-permute-start | bytes 1572872 | tf_op jit(solution)/shard_map/ppermute | solution.py:35
  52.0 11.1 %collective-permute-start.3 = (bf16[1,128,2048]{2,1,0:T(8,128)(2,1)S(1)}, bf16[1,128,2048]{2,1,0:T(8,128)(2,1)S(1)}, u32[]{:S(2)}, u32[]{:S(2)}) collective-permute-start(bf16[1,128,2048]{2,1,0:T(8,128)(2,1)S(1)} %collective-permute-done.1), channel_id=1, source_target_pairs={{0,1},{1,2},{2,3},{3,0},{4,5},{5,6},{6,7},{7,4},{8,9},{9,10},{10,1... | collective-permute-start | bytes 1572872 | tf_op jit(solution)/shard_map/ppermute | solution.py:27
  170.1 4.5 %copy-start.1 = (bf16[1,128,1024]{2,1,0:T(8,128)(2,1)S(1)}, bf16[1,128,1024]{2,1,0:T(8,128)(2,1)}, u32[]{:S(2)}) copy-start(bf16[1,128,1024]{2,1,0:T(8,128)(2,1)} %param.8) | copy-start | bytes 786436
  292.4 4.8 %copy-start.2 = (bf16[8192,256]{1,0:T(8,128)(2,1)S(1)}, bf16[8192,256]{1,0:T(8,128)(2,1)}, u32[]{:S(2)}) copy-start(bf16[8192,256]{1,0:T(8,128)(2,1)} %all-gather.5.cloned.1.call-done) | copy-start | bytes 12582916
  297.2 10.7 %copy-start = (f32[8192,64,8]{0,1,2:T(8,128)}, f32[8192,64,8]{0,1,2:T(8,128)S(1)}, u32[]{:S(2)}) copy-start(f32[8192,64,8]{0,1,2:T(8,128)S(1)} %get-tuple-element.15) | copy-start | bytes 50331652
Sparse Core Ops, SparseCore 0:
  10.1 159.9 all-gather.2
  174.8 117.5 all-gather.4
